TPU v7x, 128 devices: a whole 4x4x4 slice. The times are simulated.
128 devices in a mesh: seq: 4 (over x), rows: 8 (over z, core), expert: 4 (over y).
Axes of the slice: x: 4, y: 4, z: 4, core: 2. Of those that a mesh axis runs over, the one named last changes fastest.
Arguments:
- queries: bfloat16 [64, 6144], P(('rows', 'expert')), may hold values from -8 to 8
- k_cache: bfloat16 [64, 3072, 1024], P(('rows', 'expert'), 'seq'), may hold values from -12 to 12
- v_cache: bfloat16 [64, 3072, 1024], P(('rows', 'expert'), 'seq'), may hold values from -6 to 6
- k_new: bfloat16 [64, 1024], P(('rows', 'expert')), may hold values from -10 to 10
- v_new: bfloat16 [64, 1024], P(('rows', 'expert')), may hold values from -6 to 6
- lengths: int32 [64], P(('rows', 'expert')), may hold values from 2 to 3072, as said below
- residual: bfloat16 [64, 6144], P(('rows', 'expert')), may hold values from -60 to 60
- norm_gain: float32 [6144], replicated, may hold values from 0.1 to 1.9
- expert_ids: int32 [64, 2], P(('rows', 'expert')), may hold values from 0 to 3, all different within a row; in each aligned block of 2 rows (0 to 1, 2 to 3, ...) at most 2 rows name the same one
- combine_weights: float32 [64, 2], P(('rows', 'expert')), may hold values from 0.2 to 1
- w_gate: bfloat16 [4, 6144, 16384], P('expert', None, ('seq', 'rows')), may hold values from -0.078125 to 0.078125
- w_up: bfloat16 [4, 6144, 16384], P('expert', None, ('seq', 'rows')), may hold values from -0.078125 to 0.078125
- w_down: bfloat16 [4, 16384, 6144], P('expert', ('seq', 'rows')), may hold values from -0.046875 to 0.046875
Outputs:
- hidden_state: bfloat16 [64, 6144], P(('rows', 'expert'), 'seq')
- layer_out: bfloat16 [64, 6144], P(('rows', 'expert'), 'seq')
Inputs may be any that keep to these rules, and one draw needn't show every extreme that they name: `lengths`: the new token is not among them. `expert_ids`: each row names two different experts; within the rows of one group of seq devices (aligned blocks of 2 rows) an expert is named by at most 2 rows.
All inputs are finite; a program needn't handle non-finite values.
Results may differ from a plain program's by a relative error of at most 0.011.
Values may be sent and summed in bfloat16 or wider, within the bound.
No kernel may reach another device: no remote copies, remote signals or barrier semaphores. Data moves between devices by JAX's collectives and lax.ppermute only.
A program may use at most 128 MiB of HBM per device.

v0:
```python
import jax
import jax.numpy as jnp
from jax import lax
from jax.sharding import PartitionSpec as P

HEADS = 48
KV_HEADS = 8
HEAD_DIM = 128


def body(
    queries,
    k_cache,
    v_cache,
    k_new,
    v_new,
    lengths,
    residual,
    norm_gain,
    expert_ids,
    combine_weights,
    w_gate,
    w_up,
    w_down,
):
    rows_here, width = queries.shape
    ctx_here = k_cache.shape[1]
    groups = HEADS // KV_HEADS
    factor = HEAD_DIM ** (-0.5)
    query_heads = queries.reshape(rows_here, KV_HEADS, groups, HEAD_DIM)
    key_heads = k_cache.reshape(rows_here, ctx_here, KV_HEADS, HEAD_DIM)
    value_heads = v_cache.reshape(rows_here, ctx_here, KV_HEADS, HEAD_DIM)
    scores = (
        jnp.einsum("rhgd,rchd->rhgc", query_heads, key_heads, preferred_element_type=jnp.float32)
        * factor
    )
    position = lax.axis_index("seq") * ctx_here + jnp.arange(ctx_here, dtype=jnp.int32)
    valid = (position[None, :] < lengths[:, None])[:, None, None, :]
    local_max = jnp.max(jnp.where(valid, scores, -1e30), axis=-1)
    weights = jnp.where(valid, jnp.exp(scores - local_max[..., None]), 0.0)
    local_sum = jnp.sum(weights, axis=-1)
    local_acc = jnp.einsum(
        "rhgc,rchd->rhgd",
        weights.astype(jnp.bfloat16),
        value_heads,
        preferred_element_type=jnp.float32,
    )
    cache_max = lax.pmax(local_max, "seq")
    rescale = jnp.exp(local_max - cache_max)
    cache_sum, cache_acc = (
        lax.psum((local_sum * rescale).astype(jnp.bfloat16), "seq").astype(jnp.float32),
        lax.psum((local_acc * rescale[..., None]).astype(jnp.bfloat16), "seq").astype(jnp.float32),
    )
    own = (
        jnp.einsum(
            "rhgd,rhd->rhg",
            query_heads,
            k_new.reshape(rows_here, KV_HEADS, HEAD_DIM),
            preferred_element_type=jnp.float32,
        )
        * factor
    )
    peak = jnp.maximum(cache_max, own)
    old_scale = jnp.exp(cache_max - peak)
    fresh = jnp.exp(own - peak)
    denom = cache_sum * old_scale + fresh
    value_own = v_new.reshape(rows_here, KV_HEADS, 1, HEAD_DIM).astype(jnp.float32)
    numer = cache_acc * old_scale[..., None] + fresh[..., None] * value_own
    attn = (numer / denom[..., None]).reshape(rows_here, width)
    hidden_state = (residual.astype(jnp.float32) + attn).astype(jnp.bfloat16)
    hidden_f = hidden_state.astype(jnp.float32)
    mean_sq = jnp.mean(hidden_f * hidden_f, axis=-1, keepdims=True)
    normed = (hidden_f * lax.rsqrt(mean_sq + 1e-05) * norm_gain).astype(jnp.bfloat16)
    n_expert = lax.axis_size("expert")
    n_rows = lax.axis_size("rows")
    sources = n_rows * n_expert
    chosen = (expert_ids[:, :, None] == jnp.arange(n_expert, dtype=jnp.int32)).astype(jnp.int32)
    per_row = jnp.sum(chosen, axis=1)
    earlier = jnp.cumsum(per_row, axis=0) - per_row
    slot = jnp.sum(chosen * earlier[:, None, :], axis=-1)
    slot_hot = (slot[:, :, None] == jnp.arange(rows_here, dtype=jnp.int32)).astype(jnp.int32)
    placed = chosen[:, :, :, None] * slot_hot[:, :, None, :]
    place_rows = jnp.sum(placed, axis=1).astype(jnp.bfloat16)
    send_slots = jnp.einsum(
        "rec,rd->ecd", place_rows, normed, preferred_element_type=jnp.float32
    ).astype(jnp.bfloat16)
    everything = lax.all_gather(send_slots, ("rows", "expert"), axis=0, tiled=True)
    everything = everything.reshape(sources, n_expert, rows_here, width)
    arrived = lax.dynamic_index_in_dim(everything, lax.axis_index("expert"), 1, keepdims=False)
    slab = arrived.reshape(sources * rows_here, width)
    gate = jnp.dot(slab, w_gate[0], preferred_element_type=jnp.float32)
    upper = jnp.dot(slab, w_up[0], preferred_element_type=jnp.float32)
    act = (jax.nn.silu(gate) * upper).astype(jnp.bfloat16)
    partial_out = jnp.dot(act, w_down[0], preferred_element_type=jnp.float32)
    part_width = width // lax.axis_size("seq")
    col_start = lax.axis_index("seq") * part_width
    summed = lax.psum(partial_out.astype(jnp.bfloat16), ("seq", "rows")).astype(jnp.float32)
    summed = summed.reshape(n_rows, n_expert * rows_here, width)
    summed = lax.dynamic_index_in_dim(summed, lax.axis_index("rows"), 0, keepdims=False)
    summed = lax.dynamic_slice_in_dim(summed, col_start, part_width, 1)
    results = summed.astype(jnp.bfloat16).reshape(n_expert, rows_here, part_width)
    returned = lax.all_to_all(results, "expert", split_axis=0, concat_axis=0, tiled=True)
    mix_weights = jnp.einsum("rt,rtec->rec", combine_weights, placed.astype(jnp.float32))
    mixture = jnp.einsum("rec,ecd->rd", mix_weights, returned.astype(jnp.float32))
    hidden_part = lax.dynamic_slice_in_dim(hidden_state, col_start, part_width, 1)
    layer_out = (hidden_part.astype(jnp.float32) + mixture).astype(jnp.bfloat16)
    return (hidden_part, layer_out)


def solution(mesh):
    in_specs = (
        P(("rows", "expert"), None),
        P(("rows", "expert"), "seq", None),
        P(("rows", "expert"), "seq", None),
        P(("rows", "expert"), None),
        P(("rows", "expert"), None),
        P(("rows", "expert")),
        P(("rows", "expert"), None),
        P(),
        P(("rows", "expert"), None),
        P(("rows", "expert"), None),
        P("expert", None, ("seq", "rows")),
        P("expert", None, ("seq", "rows")),
        P("expert", ("seq", "rows"), None),
    )
    out_specs = (P(("rows", "expert"), "seq"), P(("rows", "expert"), "seq"))
    return jax.shard_map(body, mesh=mesh, in_specs=in_specs, out_specs=out_specs, check_vma=False)
```

profile of v0, /device:TPU:0, one launch (start us, length us, event | category | flops | bytes accessed | tf_op | source)
XLA Modules:
  0.0 238.7 jit_solution(8863338741338087295)
XLA Ops:
  7.2 0.0 copy-start
  7.2 0.0 all-gather.2.cloned.1.call-start
  7.2 0.9 fusion.59
  8.1 0.7 fusion.55
  8.9 0.9 select_reduce_fusion.1
  9.8 0.1 compare_convert_fusion
  9.9 0.7 multiply_convert_fusion.1
  10.6 0.5 convert_element_type.95
  11.1 0.7 reshape.123
  11.8 0.7 convert_bitcast_fusion
  12.5 0.6 copy.68
  13.1 0.8 reshape.106
  13.9 0.0 copy-start.1
  13.9 0.7 broadcast_compare_fusion
  14.6 0.0 copy-done.1
  14.6 0.7 fusion.62
  15.4 0.0 copy-done
  15.4 1.8 select_reduce_fusion
  17.1 0.0 copy-done.2
  17.1 10.7 %pmax.7 = f32[2,8,6]{2,1,0:T(8,128)S(1)} all-reduce(f32[2,8,6]{2,1,0:T(8,128)S(1)} %get-tuple-element.13), channel_id=1, replica_groups=mesh['seq'=4,'rows'=8,'expert'=4] {'seq'}, use_global_device_ids=true, to_apply=%region_1.2 | all-reduce | flops 96 | bytes 768 | tf_op jit(solution)/shard_map/pmax | solution.py:48
  27.8 0.9 fusion.31
  28.7 0.6 multiply_convert_fusion
  29.3 3.2 %fusion.26 = bf16[2,8,6,128]{3,2,1,0:T(8,128)(2,1)} fusion(f32[2,8,6,768]{3,2,1,0:T(8,128)S(1)} %get-tuple-element.14, f32[2,8,6]{2,1,0:T(8,128)S(1)} %get-tuple-element.13, pred[2,768]{1,0:T(4,128)(4,1)} %copy-done.2, f32[2,8,6]{2,1,0:T(8,128)S(1)} %get-tuple-element.10, bf16[2,768,1024]{2,1,0:T(8,128)(2,1)} %param.15), kind=kOutput, calls=%fused_computation.21 | convolution fusion | flops 19120128 | bytes 3467520 | tf_op jit(solution)/shard_map/rhgc,rchd->rhgd/dot_general | solution.py:42
  32.5 15.1 %all-reduce = (bf16[2,8,6,128]{3,2,1,0:T(8,128)(2,1)S(1)}, bf16[2,8,6]{2,1,0:T(8,128)(2,1)S(1)}) all-reduce(bf16[2,8,6,128]{3,2,1,0:T(8,128)(2,1)} %fusion.26, bf16[2,8,6]{2,1,0:T(8,128)(2,1)} %get-tuple-element.9), channel_id=1, replica_groups=mesh['seq'=4,'rows'=8,'expert'=4] {'seq'}, use_global_device_ids=true, to_apply=%region_2.3 | all-reduce | flops 12384 | bytes 49536 | tf_op jit(solution)/shard_map/psum | solution.py:52
  47.6 0.7 multiply_add_fusion
  48.4 0.8 add_divide_fusion
  49.2 0.9 fusion.43
  50.1 1.0 convolution_convert_fusion.1
  51.1 0.7 copy.29
  51.9 0.0 all-gather.2.cloned.1.call-update
  51.9 0.0 all-reduce.3.cloned.1.call-start
  52.0 46.6 %all-gather.2.cloned.1.call-done = bf16[128,2,6144]{2,1,0:T(2,128)(2,1)} async-done(((bf16[4,2,6144]{2,1,0:T(2,128)(2,1)}), bf16[128,2,6144]{2,1,0:T(2,128)(2,1)}) %all-gather.2.cloned.1.call-update) | async-done | bytes 3145744 | tf_op jit(solution)/shard_map/all_gather | solution.py:87
  98.6 2.6 %dynamic-slice_bitcast_fusion = bf16[32,1,2,6144]{3,2,0,1:T(2,128)(2,1)} fusion(bf16[32,4,2,6144]{3,2,1,0:T(2,128)(2,1)} %bitcast.72, s32[]{:T(128)S(6)} %select_n.26), kind=kLoop, calls=%fused_computation.22 | loop fusion | bytes 1572868
  101.2 2.9 %reshape.112 = bf16[64,6144]{1,0:T(8,128)(2,1)} reshape(bf16[32,1,2,6144]{3,2,0,1:T(2,128)(2,1)} %dynamic-slice_bitcast_fusion) | data formatting | bytes 1572864 | tf_op jit(solution)/shard_map/reshape | solution.py:90
  104.1 4.2 %fusion.4 = f32[64,512]{1,0:T(8,128)S(1)} fusion(bf16[64,6144]{1,0:T(8,128)(2,1)} %reshape.112, bf16[1,6144,512]{2,1,0:T(8,128)(2,1)} %param.23), kind=kOutput, calls=%fused_computation.6 | convolution fusion | flops 402653184 | bytes 7208960 | tf_op jit(solution)/shard_map/dot_general | solution.py:91
  108.4 0.0 copy-start.4
  108.4 0.0 copy-start.5
  108.4 8.1 %fusion = bf16[8,8,6144]{2,1,0:T(8,128)(2,1)} fusion(bf16[1,512,6144]{2,1,0:T(8,128)(2,1)} %param.25, bf16[64,6144]{1,0:T(8,128)(2,1)} %reshape.112, bf16[1,6144,512]{2,1,0:T(8,128)(2,1)} %param.24, f32[64,512]{1,0:T(8,128)S(1)} %fusion.4), kind=kOutput, calls=%fused_computation.1 | convolution fusion | flops 805896192 | bytes 14286848 | tf_op jit(solution)/shard_map/dot_general | solution.py:94
  116.5 0.0 all-reduce.3.cloned.1.call-update
  116.5 0.0 copy-start.3
  116.6 103.3 %all-reduce.3.cloned.1.call-done = bf16[8,8,6144]{2,1,0:T(8,128)(2,1)} async-done(((bf16[8,8,6144]{2,1,0:T(8,128)(2,1)}), bf16[8,8,6144]{2,1,0:T(8,128)(2,1)}) %all-reduce.3.cloned.1.call-update) | async-done | bytes 786448 | tf_op jit(solution)/shard_map/psum | solution.py:97
  219.9 0.8 convert_convert_fusion
  220.7 0.6 convert_element_type.102
  221.3 4.3 %all-to-all-start = ((bf16[4,2,1536]{2,1,0:T(2,128)(2,1)}), bf16[4,2,1536]{2,1,0:T(2,128)(2,1)S(1)}, u32[]{:S(2)}, u32[]{:S(2)}) async-start(bf16[4,2,1536]{2,1,0:T(2,128)(2,1)} %convert_element_type.102), calls=%async_computation | async-start | bytes 49152 | tf_op jit(solution)/shard_map/all_to_all | solution.py:102
  225.6 0.0 copy-done.4
  225.6 0.1 fusion.51
  225.7 5.3 %all-to-all-done = bf16[4,2,1536]{2,1,0:T(2,128)(2,1)S(1)} async-done(((bf16[4,2,1536]{2,1,0:T(2,128)(2,1)}), bf16[4,2,1536]{2,1,0:T(2,128)(2,1)S(1)}, u32[]{:S(2)}, u32[]{:S(2)}) %all-to-all-start) | async-done | bytes 24608 | tf_op jit(solution)/shard_map/all_to_all | solution.py:102
  231.0 0.8 fusion.13
  (9 shorter events, 0.1 us)
Async XLA Ops:
  7.2 8.2 %copy-start = (bf16[2,768,1024]{2,1,0:T(8,128)(2,1)S(1)}, bf16[2,768,1024]{2,1,0:T(8,128)(2,1)}, u32[]{:S(2)}) copy-start(bf16[2,768,1024]{2,1,0:T(8,128)(2,1)} %param.14) | copy-start | bytes 9437188
  7.2 91.4 %all-gather.2.cloned.1.call-start = ((), (), s32[]{:S(2)}) async-start(), calls=%async_computation.1 | async-start | bytes 3244032 | tf_op jit(solution)/shard_map/all_gather | solution.py:87
  13.9 0.8 copy-start.1
  14.6 2.5 %copy-start.2 = (pred[2,768]{1,0:T(4,128)(4,1)}, pred[2,768]{1,0:T(4,128)(4,1)S(1)}, u32[]{:S(2)}) copy-start(pred[2,768]{1,0:T(4,128)(4,1)S(1)} %broadcast_compare_fusion) | copy-start | bytes 4612
  51.9 168.0 %all-reduce.3.cloned.1.call-start = ((), (), s32[]{:S(2)}) async-start(), calls=%async_computation.2 | async-start | bytes 1572864 | tf_op jit(solution)/shard_map/psum | solution.py:97
  108.4 117.3 %copy-start.4 = (bf16[2,2,4,2]{2,3,1,0:T(2,128)(2,1)S(1)}, bf16[2,2,4,2]{2,3,1,0:T(2,128)(2,1)}, u32[]{:S(2)}) copy-start(bf16[2,2,4,2]{2,3,1,0:T(2,128)(2,1)} %get-tuple-element.11) | copy-start | bytes 196
  108.4 117.2 %copy-start.5 = (f32[2,2]{1,0:T(2,128)S(1)}, f32[2,2]{1,0:T(2,128)}, u32[]{:S(2)}) copy-start(f32[2,2]{1,0:T(2,128)} %param.22) | copy-start | bytes 52
  116.5 115.3 %copy-start.3 = (bf16[2,1536]{1,0:T(2,128)(2,1)}, bf16[2,1536]{1,0:T(2,128)(2,1)S(1)}, u32[]{:S(2)}) copy-start(bf16[2,1536]{1,0:T(2,128)(2,1)S(1)} %constant_dynamic-slice_fusion) | copy-start | bytes 18436
  221.3 9.7 %all-to-all-start = ((bf16[4,2,1536]{2,1,0:T(2,128)(2,1)}), bf16[4,2,1536]{2,1,0:T(2,128)(2,1)S(1)}, u32[]{:S(2)}, u32[]{:S(2)}) async-start(bf16[4,2,1536]{2,1,0:T(2,128)(2,1)} %convert_element_type.102), calls=%async_computation | async-start | bytes 49152 | tf_op jit(solution)/shard_map/all_to_all | solution.py:102
Sparse Core Ops, SparseCore 0:
  52.0 46.5 all-gather.1
  116.6 103.2 all-reduce.2
where the time goes:
time: 240 us; the launch traced here: 239 us
  waiting for transfers between devices  155 us (65%)
  blocking collectives  25.8 us (11%)
  matrix products  19.9 us (8%)
  between operations  14.2 us (6%)
  other arithmetic  10.1 us (4%)
  local copies, waits for them, and re-layouts  8.98 us (4%)
  starting transfers between devices  4.36 us (2%)
    psum x1, waiting for transfers between devices, body(): lax.psum(partial_out.astype(jnp.bfloat16), ('seq', 'rows'))  103 us
    all_gather x1, waiting for transfers between devices, body(): lax.all_gather(send_slots, ('rows', 'expert'), axis=0, tiled=True)  46.6 us
    psum x1, blocking collectives, body(): lax.psum((local_acc * rescale[..., None]).astype(jnp.bfloat16), 'seq')  15.1 us
    pmax x1, blocking collectives, body(): cache_max = lax.pmax(local_max, 'seq')  10.7 us
    dot_general x1, matrix products, body(): partial_out = jnp.dot(act, w_down[0], preferred_element_type=jnp.float32)  8.11 us
    all_to_all x1, waiting for transfers between devices, body(): lax.all_to_all(results, 'expert', split_axis=0, concat_axis=0, tiled=True)  5.28 us
  transfers between devices with their start and end apart: 3, of which 3 were waited for; matrix products, arithmetic and copies ran while one was open for 0% of the time, Pallas kernels for 0%

commit v1 on v0

v1 whole, which is shorter than its diff:
```python
import jax
import jax.numpy as jnp
from jax import lax
from jax.experimental import pallas as pl
from jax.experimental.pallas import tpu as pltpu
from jax.sharding import Mesh, PartitionSpec as P

HEADS = 48
KV_HEADS = 8
HEAD_DIM = 128
GROUPS = HEADS // KV_HEADS
D = HEADS * HEAD_DIM
SEQ = 4
CTX_HERE = 768
PAY = 112
FF_HERE = 512
BLK = 24
MIB = 1 << 20
NEG = -1e30


def head_masks(shape):
    line = lax.broadcasted_iota(jnp.int32, shape, 0)
    return [(line >= GROUPS * k) & (line < GROUPS * (k + 1)) for k in range(KV_HEADS)]


def spread_heads(row, masks):
    out = jnp.zeros((HEADS, HEAD_DIM), jnp.float32)
    for k in range(KV_HEADS):
        piece = jnp.broadcast_to(row[:, k * HEAD_DIM : (k + 1) * HEAD_DIM], (HEADS, HEAD_DIM))
        out = jnp.where(masks[k], piece, out)
    return out


def attention_kernel(len_ref, q_ref, kn_ref, vn_ref, k_hbm, v_hbm, out_ref, kbuf, vbuf, qs, sems):
    seq = lax.axis_index("seq")
    copies = []
    for r in range(2):
        ck = pltpu.make_async_copy(k_hbm.at[r], kbuf.at[r], sems.at[2 * r])
        cv = pltpu.make_async_copy(v_hbm.at[r], vbuf.at[r], sems.at[2 * r + 1])
        ck.start()
        cv.start()
        copies.append((ck, cv))
    factor = HEAD_DIM ** (-0.5)
    masks = head_masks((HEADS, HEAD_DIM))
    queries = q_ref[...].astype(jnp.float32)
    keys_new = kn_ref[...].astype(jnp.float32)
    values_new = vn_ref[...].astype(jnp.float32)
    line = lax.broadcasted_iota(jnp.int32, (HEADS, HEAD_DIM), 0)
    lane = lax.broadcasted_iota(jnp.int32, (HEADS, HEAD_DIM), 1)
    position = lax.broadcasted_iota(jnp.int32, (HEADS, CTX_HERE), 1) + seq * CTX_HERE
    lse_row = jnp.zeros((1, HEAD_DIM), jnp.float32)
    for r in range(2):
        for h in range(HEADS):
            qs[r * HEADS + h : r * HEADS + h + 1, :] = queries[
                r : r + 1, h * HEAD_DIM : (h + 1) * HEAD_DIM
            ]
        q = qs[r * HEADS : (r + 1) * HEADS, :]
        wide = jnp.concatenate([jnp.where(m, q, 0.0) for m in masks], axis=1).astype(jnp.bfloat16)
        own = jnp.sum(q * spread_heads(keys_new[r : r + 1], masks), axis=1, keepdims=True) * factor
        own = jnp.where(seq == 0, own, NEG)
        copies[r][0].wait()
        scores = (
            lax.dot_general(
                wide, kbuf[r], (((1,), (1,)), ((), ())), preferred_element_type=jnp.float32
            )
            * factor
        )
        valid = position < len_ref[r]
        scores = jnp.where(valid, scores, NEG)
        top = jnp.maximum(jnp.max(scores, axis=1, keepdims=True), own)
        probs = jnp.where(valid, jnp.exp(scores - top), 0.0)
        fresh = jnp.where(seq == 0, jnp.exp(own - top), 0.0)
        total = jnp.sum(probs, axis=1, keepdims=True) + fresh
        copies[r][1].wait()
        pv = jnp.dot(probs.astype(jnp.bfloat16), vbuf[r], preferred_element_type=jnp.float32)
        acc = fresh * spread_heads(values_new[r : r + 1], masks)
        for k in range(KV_HEADS):
            acc = acc + jnp.where(masks[k], pv[:, k * HEAD_DIM : (k + 1) * HEAD_DIM], 0.0)
        some = total > 0.0
        safe = jnp.where(some, total, 1.0)
        lse = jnp.where(some, top + jnp.log(safe), NEG)
        out_ref[r * HEADS : (r + 1) * HEADS, :] = (acc / safe).astype(jnp.bfloat16)
        lse_row = lse_row + jnp.sum(
            jnp.where(lane == line + r * HEADS, lse, 0.0), axis=0, keepdims=True
        )
    hi = lse_row.astype(jnp.bfloat16).astype(jnp.float32)
    mid = (lse_row - hi).astype(jnp.bfloat16).astype(jnp.float32)
    low = lse_row - hi - mid
    tail = lax.broadcasted_iota(jnp.int32, (16, HEAD_DIM), 0)
    tile = jnp.where(tail == 0, hi, jnp.where(tail == 1, mid, jnp.where(tail == 2, low, 0.0)))
    out_ref[2 * HEADS : PAY, :] = tile.astype(jnp.bfloat16)


def combine_kernel(ids_ref, cw_ref, p0, p1, p2, p3, res_ref, pay_ref, hid_ref, rs):
    seq = lax.axis_index("seq")
    residual = res_ref[...].astype(jnp.float32)
    for r in range(2):
        for h in range(HEADS):
            rs[r * HEADS + h : r * HEADS + h + 1, :] = residual[
                r : r + 1, h * HEAD_DIM : (h + 1) * HEAD_DIM
            ]
    line = lax.broadcasted_iota(jnp.int32, (2 * HEADS, HEAD_DIM), 0)
    lane = lax.broadcasted_iota(jnp.int32, (2 * HEADS, HEAD_DIM), 1)
    lses, outs = [], []
    for ref in (p0, p1, p2, p3):
        outs.append(ref[0 : 2 * HEADS, :].astype(jnp.float32))
        side = ref[2 * HEADS : PAY, :].astype(jnp.float32)
        row = side[0:1, :] + side[1:2, :] + side[2:3, :]
        lses.append(jnp.sum(jnp.where(lane == line, row, 0.0), axis=1, keepdims=True))
    top = jnp.maximum(jnp.maximum(lses[0], lses[1]), jnp.maximum(lses[2], lses[3]))
    scales = [jnp.exp(v - top) for v in lses]
    total = (scales[0] + scales[1]) + (scales[2] + scales[3])
    acc = (scales[0] * outs[0] + scales[1] * outs[1]) + (scales[2] * outs[2] + scales[3] * outs[3])
    hidden = (rs[...] + acc / total).astype(jnp.bfloat16)
    rs[...] = hidden.astype(jnp.float32)
    tail = lax.broadcasted_iota(jnp.int32, (16, HEAD_DIM), 0)
    tail_lane = lax.broadcasted_iota(jnp.int32, (16, HEAD_DIM), 1)
    mix = jnp.zeros((16, HEAD_DIM), jnp.float32)
    for r in range(2):
        for t in range(2):
            expert = ids_ref[r, t]
            here = (tail == r) & ((tail_lane == expert) | (tail_lane == expert + 4))
            mix = jnp.where(here, cw_ref[r, t], mix)
    coarse = mix.astype(jnp.bfloat16).astype(jnp.float32)
    side = jnp.where(tail_lane < 4, coarse, mix - coarse).astype(jnp.bfloat16)
    for j in range(16):
        pay_ref[j, 0 : 2 * HEADS, :] = hidden
        pay_ref[j, 2 * HEADS : PAY, :] = side
    rows = []
    for r in range(2):
        first = r * HEADS + seq * (HEADS // SEQ)
        rows.append(
            jnp.concatenate([rs[pl.ds(first + c, 1), :] for c in range(HEADS // SEQ)], axis=1)
        )
    hid_ref[...] = jnp.concatenate(rows, axis=0).astype(jnp.bfloat16)


def expert_kernel(
    xa, xb, gain_ref, wg_hbm, wu_hbm, wd_hbm, own_ref, sib_ref, wg, wu, wd, flat, lhs, mt, sems
):
    expert = lax.axis_index("expert")
    parts = 6
    kc = D // parts
    gates, ups, downs = [], [], []
    for i in range(parts):
        span = pl.ds(i * kc, kc)
        gates.append(pltpu.make_async_copy(wg_hbm.at[0, span], wg.at[span], sems.at[0, i]))
        ups.append(pltpu.make_async_copy(wu_hbm.at[0, span], wu.at[span], sems.at[1, i]))
        downs.append(pltpu.make_async_copy(wd_hbm.at[0, :, span], wd.at[:, span], sems.at[2, i]))
    for i in range(parts):
        gates[i].start()
        ups[i].start()
    for i in range(parts):
        downs[i].start()
    for half, ref in enumerate((xa, xb)):
        for j in range(16):
            first = (half * 32 + j * 2) * HEADS
            flat[first : first + 2 * HEADS, :] = ref[j, 0 : 2 * HEADS, :].astype(jnp.float32)
            mt[half * 32 + 2 * j : half * 32 + 2 * j + 2, :] = ref[
                j, 2 * HEADS : PAY, :
            ].astype(jnp.float32)[0:2]
    squares = jnp.zeros((64, HEAD_DIM), jnp.float32)
    for h in range(HEADS):
        x = flat[pl.ds(h, 64, stride=HEADS), :]
        squares = squares + x * x
        lhs[:, h * HEAD_DIM : (h + 1) * HEAD_DIM] = (x * gain_ref[h : h + 1, :]).astype(jnp.bfloat16)
    scale = lax.rsqrt(jnp.sum(squares, axis=1, keepdims=True) * (1.0 / D) + 1e-05)
    lane = lax.broadcasted_iota(jnp.int32, (64, HEAD_DIM), 1)
    mine = (lane == expert) | (lane == expert + 4)
    weight = jnp.sum(jnp.where(mine, mt[...], 0.0), axis=1, keepdims=True)
    gate = jnp.zeros((64, FF_HERE), jnp.float32)
    upper = jnp.zeros((64, FF_HERE), jnp.float32)
    for i in range(parts):
        x = lhs[:, i * kc : (i + 1) * kc]
        gates[i].wait()
        gate = gate + jnp.dot(x, wg[i * kc : (i + 1) * kc, :], preferred_element_type=jnp.float32)
        ups[i].wait()
        upper = upper + jnp.dot(x, wu[i * kc : (i + 1) * kc, :], preferred_element_type=jnp.float32)
    gate = gate * scale
    upper = upper * scale
    act = (gate / (1.0 + jnp.exp(-gate)) * upper).astype(jnp.bfloat16)
    for i in range(parts):
        downs[i].wait()
        out = (
            jnp.dot(act, wd[:, i * kc : (i + 1) * kc], preferred_element_type=jnp.float32) * weight
        )
        for g in range(kc // HEAD_DIM):
            place = i * (kc // HEAD_DIM) + g
            first = (place // 12) * (16 * BLK) + place % 12
            piece = out[:, g * HEAD_DIM : (g + 1) * HEAD_DIM]
            flat[pl.ds(first, 32, stride=12), :] = piece[0:32]
            flat[pl.ds(64 * BLK + first, 32, stride=12), :] = piece[32:64]
    own_ref[...] = flat[0 : 64 * BLK, :].astype(jnp.bfloat16)
    sib_ref[...] = flat[64 * BLK : 128 * BLK, :].astype(jnp.bfloat16)


def finish_kernel(parts_ref, hid_ref, out_ref):
    total = jnp.zeros((BLK, HEAD_DIM), jnp.float32)
    for j in range(64):
        total = total + parts_ref[j].astype(jnp.float32)
    rows = [
        jnp.concatenate([total[r * 12 + c : r * 12 + c + 1, :] for c in range(12)], axis=1)
        for r in range(2)
    ]
    mixture = jnp.concatenate(rows, axis=0)
    out_ref[...] = (hid_ref[...].astype(jnp.float32) + mixture).astype(jnp.bfloat16)


VMEM = pl.BlockSpec(memory_space=pltpu.VMEM)
SMEM = pl.BlockSpec(memory_space=pltpu.SMEM)
ANY = pl.BlockSpec(memory_space=pl.ANY)


def params(mib):
    return pltpu.CompilerParams(vmem_limit_bytes=mib * MIB)


def body(
    queries,
    k_cache,
    v_cache,
    k_new,
    v_new,
    lengths,
    residual,
    norm_gain,
    expert_ids,
    combine_weights,
    w_gate,
    w_up,
    w_down,
):
    bf16, f32 = jnp.bfloat16, jnp.float32
    partial = pl.pallas_call(
        attention_kernel,
        out_shape=jax.ShapeDtypeStruct((PAY, HEAD_DIM), bf16),
        in_specs=[SMEM, VMEM, VMEM, VMEM, ANY, ANY],
        out_specs=VMEM,
        scratch_shapes=[
            pltpu.VMEM((2, CTX_HERE, KV_HEADS * HEAD_DIM), bf16),
            pltpu.VMEM((2, CTX_HERE, KV_HEADS * HEAD_DIM), bf16),
            pltpu.VMEM((2 * HEADS, HEAD_DIM), f32),
            pltpu.SemaphoreType.DMA((4,)),
        ],
        compiler_params=params(16),
        name="attention",
    )(lengths, queries, k_new, v_new, k_cache, v_cache)
    others = [
        lax.ppermute(partial, "seq", [(i, (i + k) % SEQ) for i in range(SEQ)]) for k in (1, 3, 2)
    ]
    pay, hidden_part = pl.pallas_call(
        combine_kernel,
        out_shape=(
            jax.ShapeDtypeStruct((16, PAY, HEAD_DIM), bf16),
            jax.ShapeDtypeStruct((2, D // SEQ), bf16),
        ),
        in_specs=[SMEM, SMEM] + [VMEM] * 5,
        out_specs=(VMEM, VMEM),
        scratch_shapes=[pltpu.VMEM((2 * HEADS, HEAD_DIM), f32)],
        compiler_params=params(8),
        name="combine",
    )(expert_ids, combine_weights, partial, *others, residual)
    mine = lax.all_to_all(pay, ("z", "expert"), 0, 0, tiled=True)
    theirs = lax.ppermute(mine, "core", [(0, 1), (1, 0)])
    own_out, sib_out = pl.pallas_call(
        expert_kernel,
        out_shape=(
            jax.ShapeDtypeStruct((64 * BLK, HEAD_DIM), bf16),
            jax.ShapeDtypeStruct((64 * BLK, HEAD_DIM), bf16),
        ),
        in_specs=[VMEM, VMEM, VMEM, ANY, ANY, ANY],
        out_specs=(VMEM, VMEM),
        scratch_shapes=[
            pltpu.VMEM((D, FF_HERE), bf16),
            pltpu.VMEM((D, FF_HERE), bf16),
            pltpu.VMEM((FF_HERE, D), bf16),
            pltpu.VMEM((64 * HEADS, HEAD_DIM), f32),
            pltpu.VMEM((64, D), bf16),
            pltpu.VMEM((64, HEAD_DIM), f32),
            pltpu.SemaphoreType.DMA((3, 6)),
        ],
        compiler_params=params(32),
        name="experts",
    )(mine, theirs, norm_gain.reshape(HEADS, HEAD_DIM), w_gate, w_up, w_down)
    from_sib = lax.ppermute(sib_out, "core", [(0, 1), (1, 0)])
    summed = (own_out.astype(f32) + from_sib.astype(f32)).astype(bf16)
    blocks = lax.all_to_all(
        summed.reshape(64, BLK, HEAD_DIM), ("seq", "z", "expert"), 0, 0, tiled=True
    )
    layer_out = pl.pallas_call(
        finish_kernel,
        out_shape=jax.ShapeDtypeStruct((2, D // SEQ), bf16),
        in_specs=[VMEM, VMEM],
        out_specs=VMEM,
        compiler_params=params(8),
        name="finish",
    )(blocks, hidden_part)
    return hidden_part, layer_out


def solution(mesh):
    fine = Mesh(mesh.devices.reshape(4, 4, 2, 4), ("seq", "z", "core", "expert"))
    rows = ("z", "core", "expert")
    in_specs = (
        P(rows, None),
        P(rows, "seq", None),
        P(rows, "seq", None),
        P(rows, None),
        P(rows, None),
        P(rows),
        P(rows, None),
        P(),
        P(rows, None),
        P(rows, None),
        P("expert", None, ("seq", "z", "core")),
        P("expert", None, ("seq", "z", "core")),
        P("expert", ("seq", "z", "core"), None),
    )
    out_specs = (P(rows, "seq"), P(rows, "seq"))
    return jax.shard_map(body, mesh=fine, in_specs=in_specs, out_specs=out_specs, check_vma=False)
```

time: 240 us -> 73.4 us (0.31)
  waiting for transfers between devices: 155 us -> 7.59 us
  matrix products: 19.9 us -> 0 us
  between operations: 14.2 us -> 0.7 us
  Pallas kernels: 0 us -> 12.9 us
  other arithmetic: 10.1 us -> 0.1 us
  blocking collectives: 25.8 us -> 33.8 us
  local copies, waits for them, and re-layouts: 8.98 us -> 12.6 us
    psum x1 -> x0, waiting for transfers between devices: 103 us -> none  [body(): lax.psum(partial_out.astype(jnp.bfloat16), ('seq', 'rows'))]
    all_gather x1 -> x0, waiting for transfers between devices: 46.6 us -> none  [body(): lax.all_gather(send_slots, ('rows', 'expert'), axis=0, tiled=True)]
    all_to_all x0 -> x2, blocking collectives: none -> 33.8 us  [the longest x1 17.6 us: body(): mine = lax.all_to_all(pay, ('z', 'expert'), 0, 0, tiled=True)]
    dot_general x8 -> x0, matrix products: 19.9 us -> none  [the longest x1 8.11 us: body(): partial_out = jnp.dot(act, w_down[0], preferred_element_type=jnp.float32)]
    psum x1 -> x0, blocking collectives: 15.1 us -> none  [body(): lax.psum((local_acc * rescale[..., None]).astype(jnp.bfloat16), 'seq')]
    pallas_call x0 -> x4, Pallas kernels: none -> 12.9 us  [the longest x1 7.14 us: body(): pl.pallas_call(expert_kernel, out_shape=(jax.ShapeDtypeStruct((64 * BLK,...]
    pmax x1 -> x0, blocking collectives: 10.7 us -> none  [body(): cache_max = lax.pmax(local_max, 'seq')]
    unnamed x14 -> x28, local copies, waits for them, and re-layouts: 3.18 us -> 12.6 us
  transfers between devices with their start and end apart: 3 -> 5, of which waited for: 3 -> 5; matrix products, arithmetic and copies ran while one was open for 0% -> 0% of each run, Pallas kernels for 0% -> 0%
where the time goes in v1:
time: 73.4 us; the launch traced here: 73.1 us
  blocking collectives  33.8 us (46%)
  Pallas kernels  12.9 us (18%)
  local copies, waits for them, and re-layouts  12.6 us (17%)
  waiting for transfers between devices  7.59 us (10%)
  starting transfers between devices  5.43 us (7%)
    all_to_all x1, blocking collectives, body(): mine = lax.all_to_all(pay, ('z', 'expert'), 0, 0, tiled=True)  17.6 us
    all_to_all x1, blocking collectives, body(): lax.all_to_all(summed.reshape(64, BLK, HEAD_DIM), ('seq', 'z', 'expert'),...  16.2 us
    unnamed x28, local copies, waits for them, and re-layouts  12.6 us
    pallas_call x1, Pallas kernels, body(): pl.pallas_call(expert_kernel, out_shape=(jax.ShapeDtypeStruct((64 * BLK,...  7.14 us
    ppermute x3, starting transfers between devices, body(): lax.ppermute(partial, 'seq', [(i, (i + k) % SEQ) for i in range(SEQ)])  5.21 us
    ppermute x3, waiting for transfers between devices, body(): lax.ppermute(partial, 'seq', [(i, (i + k) % SEQ) for i in range(SEQ)])  4.19 us
    pallas_call x1, Pallas kernels, body(): pl.pallas_call(attention_kernel, out_shape=jax.ShapeDtypeStruct((PAY, HEA...  3.76 us
    ppermute x1, waiting for transfers between devices, body(): theirs = lax.ppermute(mine, 'core', [(0, 1), (1, 0)])  1.81 us
  transfers between devices with their start and end apart: 5, of which 5 were waited for; matrix products, arithmetic and copies ran while one was open for 0% of the time, Pallas kernels for 0%

profile of v1, /device:TPU:0, one launch (start us, length us, event | category | flops | bytes accessed | tf_op | source)
XLA Modules:
  0.0 73.1 jit_solution(10231677131010589973)
XLA Ops:
  0.6 0.0 copy-start
  0.6 0.0 copy-start.3
  0.7 2.0 %copy-done.3 = bf16[2,768,1024]{2,1,0:T(8,128)(2,1)S(1)} copy-done((bf16[2,768,1024]{2,1,0:T(8,128)(2,1)S(1)}, bf16[2,768,1024]{2,1,0:T(8,128)(2,1)}, u32[]{:S(2)}) %copy-start.3) | copy-done | bytes 3145752
  2.7 0.0 copy-start.4
  2.7 2.1 %copy-done.4 = bf16[2,768,1024]{2,1,0:T(8,128)(2,1)S(1)} copy-done((bf16[2,768,1024]{2,1,0:T(8,128)(2,1)S(1)}, bf16[2,768,1024]{2,1,0:T(8,128)(2,1)}, u32[]{:S(2)}) %copy-start.4) | copy-done | bytes 3145752
  4.8 0.0 copy-start.5
  4.8 0.7 %copy-done.5 = bf16[2,6144]{1,0:T(2,128)(2,1)S(1)} copy-done((bf16[2,6144]{1,0:T(2,128)(2,1)S(1)}, bf16[2,6144]{1,0:T(2,128)(2,1)}, u32[]{:S(2)}) %copy-start.5) | copy-done | bytes 24600
  5.6 0.0 copy-start.9
  5.6 0.7 copy-done.9
  6.3 0.0 copy-start.10
  6.3 0.7 copy-done.10
  6.9 0.0 copy-start.13
  7.0 0.7 copy-done.13
  7.6 0.0 copy-start.6
  7.6 0.0 copy-start.11
  7.6 0.0 copy-start.12
  7.6 0.0 copy-start.7
  7.6 3.8 %attention.1.p0 = bf16[112,128]{1,0:T(8,128)(2,1)S(1)} custom-call(s32[2]{0:T(128)S(1)} %copy-done.13, bf16[2,6144]{1,0:T(2,128)(2,1)S(1)} %copy-done.5, bf16[2,1024]{1,0:T(2,128)(2,1)S(1)} %copy-done.9, bf16[2,1024]{1,0:T(2,128)(2,1)S(1)} %copy-done.10, bf16[2,768,1024]{2,1,0:T(8,128)(2,1)S(1)} %copy-done.3, bf16[2,768,1024]{2,1,0:T(8,128)(2,1)S(1)} %copy-done.4), custom_call_target="tpu_custom_call" | custom-call | tf_op jit(solution)/shard_map/attention/pallas_call | solution.py:235
  11.4 3.2 %collective-permute-start.2 = (bf16[112,128]{1,0:T(8,128)(2,1)S(1)}, bf16[112,128]{1,0:T(8,128)(2,1)S(1)}, u32[]{:S(2)}, u32[]{:S(2)}) collective-permute-start(bf16[112,128]{1,0:T(8,128)(2,1)S(1)} %attention.1.p0), channel_id=1, source_target_pairs={{0,64},{32,96},{64,0},{96,32},{1,65},{33,97},{65,1},{97,33},{2,66}... | collective-permute-start | bytes 86024 | tf_op jit(solution)/shard_map/ppermute | solution.py:250
  14.6 1.1 %collective-permute-start.1 = (bf16[112,128]{1,0:T(8,128)(2,1)S(1)}, bf16[112,128]{1,0:T(8,128)(2,1)S(1)}, u32[]{:S(2)}, u32[]{:S(2)}) collective-permute-start(bf16[112,128]{1,0:T(8,128)(2,1)S(1)} %attention.1.p0), channel_id=1, source_target_pairs={{0,96},{32,0},{64,32},{96,64},{1,97},{33,1},{65,33},{97,65},{2,98}... | collective-permute-start | bytes 86024 | tf_op jit(solution)/shard_map/ppermute | solution.py:250
  15.7 0.9 %collective-permute-start = (bf16[112,128]{1,0:T(8,128)(2,1)S(1)}, bf16[112,128]{1,0:T(8,128)(2,1)S(1)}, u32[]{:S(2)}, u32[]{:S(2)}) collective-permute-start(bf16[112,128]{1,0:T(8,128)(2,1)S(1)} %attention.1.p0), channel_id=1, source_target_pairs={{0,32},{32,64},{64,96},{96,0},{1,33},{33,65},{65,97},{97,1},{2,34}... | collective-permute-start | bytes 86024 | tf_op jit(solution)/shard_map/ppermute | solution.py:250
  16.6 0.2 collective-permute-done.2.p3
  16.8 1.6 %collective-permute-done.1.p2 = bf16[112,128]{1,0:T(8,128)(2,1)S(1)} collective-permute-done((bf16[112,128]{1,0:T(8,128)(2,1)S(1)}, bf16[112,128]{1,0:T(8,128)(2,1)S(1)}, u32[]{:S(2)}, u32[]{:S(2)}) %collective-permute-start.1) | collective-permute-done | bytes 28704 | tf_op jit(solution)/shard_map/ppermute | solution.py:250
  18.4 2.4 %collective-permute-done.p1 = bf16[112,128]{1,0:T(8,128)(2,1)S(1)} collective-permute-done((bf16[112,128]{1,0:T(8,128)(2,1)S(1)}, bf16[112,128]{1,0:T(8,128)(2,1)S(1)}, u32[]{:S(2)}, u32[]{:S(2)}) %collective-permute-start) | collective-permute-done | bytes 28704 | tf_op jit(solution)/shard_map/ppermute | solution.py:250
  20.8 0.0 copy-done.6
  20.8 0.0 copy-done.11
  20.8 0.0 copy-done.12
  20.8 1.4 %combine.1 = (bf16[16,112,128]{2,1,0:T(8,128)(2,1)S(1)}, bf16[2,1536]{1,0:T(2,128)(2,1)}) custom-call(s32[2,2]{1,0:T(2,128)S(1)} %copy-done.11, f32[2,2]{1,0:T(2,128)S(1)} %copy-done.12, bf16[112,128]{1,0:T(8,128)(2,1)S(1)} %attention.1.p0, bf16[112,128]{1,0:T(8,128)(2,1)S(1)} %collective-permute-done.p1, bf16[112,128]{1,0:T(8,128)(2,1)S(1)} %collective-permute-done.1.p2, ...), custom_call_target="tpu_custom_call" | custom-call | tf_op jit(solution)/shard_map/combine/pallas_call | solution.py:252
  22.2 17.6 %all_to_all.10.xa = bf16[16,112,128]{2,1,0:T(8,128)(2,1)S(1)} all-to-all(bf16[16,112,128]{2,1,0:T(8,128)(2,1)S(1)} %get-tuple-element.7), channel_id=1, replica_groups=mesh['seq'=4,'z'=4,'core'=2,'expert'=4] {'z','expert'}, dimensions={0} | all-to-all | bytes 917504 | tf_op jit(solution)/shard_map/all_to_all | solution.py:264
  39.7 0.0 collective-permute-start.3
  39.7 1.8 %collective-permute-done.3.xb = bf16[16,112,128]{2,1,0:T(8,128)(2,1)S(1)} collective-permute-done((bf16[16,112,128]{2,1,0:T(8,128)(2,1)S(1)}, bf16[16,112,128]{2,1,0:T(8,128)(2,1)S(1)}, u32[]{:S(2)}, u32[]{:S(2)}) %collective-permute-start.3) | collective-permute-done | bytes 458784 | tf_op jit(solution)/shard_map/ppermute | solution.py:265
  41.6 0.0 copy-done
  41.6 0.0 copy-done.7
  41.6 0.0 copy-start.1
  41.6 2.8 %copy-done.1 = bf16[1,6144,512]{2,1,0:T(8,128)(2,1)S(1)} copy-done((bf16[1,6144,512]{2,1,0:T(8,128)(2,1)S(1)}, bf16[1,6144,512]{2,1,0:T(8,128)(2,1)}, u32[]{:S(2)}) %copy-start.1) | copy-done | bytes 6291480
  44.4 0.0 copy-start.2
  44.4 2.8 %copy-done.2 = bf16[1,512,6144]{2,1,0:T(8,128)(2,1)S(1)} copy-done((bf16[1,512,6144]{2,1,0:T(8,128)(2,1)S(1)}, bf16[1,512,6144]{2,1,0:T(8,128)(2,1)}, u32[]{:S(2)}) %copy-start.2) | copy-done | bytes 6291480
  47.2 0.0 copy-start.8
  47.2 7.1 %experts.1 = (bf16[1536,128]{1,0:T(8,128)(2,1)S(1)}, bf16[1536,128]{1,0:T(8,128)(2,1)S(1)}) custom-call(bf16[16,112,128]{2,1,0:T(8,128)(2,1)S(1)} %all_to_all.10.xa, bf16[16,112,128]{2,1,0:T(8,128)(2,1)S(1)} %collective-permute-done.3.xb, f32[48,128]{1,0:T(8,128)S(1)} %bitcast.2, bf16[1,6144,512]{2,1,0:T(8,128)(2,1)S(1)} %copy-done, ...), custom_call_target="tpu_custom_call" | custom-call | tf_op jit(solution)/shard_map/experts/pallas_call | solution.py:266
  54.3 0.2 collective-permute-start.4
  54.5 1.6 %collective-permute-done.4 = bf16[1536,128]{1,0:T(8,128)(2,1)S(1)} collective-permute-done((bf16[1536,128]{1,0:T(8,128)(2,1)S(1)}, bf16[1536,128]{1,0:T(8,128)(2,1)S(1)}, u32[]{:S(2)}, u32[]{:S(2)}) %collective-permute-start.4) | collective-permute-done | bytes 393248 | tf_op jit(solution)/shard_map/ppermute | solution.py:286
  56.1 0.1 add_convert_fusion
  56.2 16.2 %all_to_all.11.parts_ref = bf16[64,24,128]{2,1,0:T(8,128)(2,1)S(1)} all-to-all(bf16[64,24,128]{2,1,0:T(8,128)(2,1)S(1)} %bitcast.3), channel_id=1, replica_groups=mesh['seq'=4,'z'=4,'core'=2,'expert'=4] {'seq','z','expert'}, dimensions={0} | all-to-all | bytes 786432 | tf_op jit(solution)/shard_map/all_to_all | solution.py:288
  72.4 0.0 copy-done.8
  72.4 0.7 finish.1
Async XLA Ops:
  0.6 40.9 %copy-start = (bf16[1,6144,512]{2,1,0:T(8,128)(2,1)S(1)}, bf16[1,6144,512]{2,1,0:T(8,128)(2,1)}, u32[]{:S(2)}) copy-start(bf16[1,6144,512]{2,1,0:T(8,128)(2,1)} %wg_hbm.1) | copy-start | bytes 18874372
  0.6 2.0 %copy-start.3 = (bf16[2,768,1024]{2,1,0:T(8,128)(2,1)S(1)}, bf16[2,768,1024]{2,1,0:T(8,128)(2,1)}, u32[]{:S(2)}) copy-start(bf16[2,768,1024]{2,1,0:T(8,128)(2,1)} %k_hbm.1) | copy-start | bytes 9437188
  2.7 2.2 %copy-start.4 = (bf16[2,768,1024]{2,1,0:T(8,128)(2,1)S(1)}, bf16[2,768,1024]{2,1,0:T(8,128)(2,1)}, u32[]{:S(2)}) copy-start(bf16[2,768,1024]{2,1,0:T(8,128)(2,1)} %v_hbm.1) | copy-start | bytes 9437188
  4.8 0.7 %copy-start.5 = (bf16[2,6144]{1,0:T(2,128)(2,1)S(1)}, bf16[2,6144]{1,0:T(2,128)(2,1)}, u32[]{:S(2)}) copy-start(bf16[2,6144]{1,0:T(2,128)(2,1)} %q_ref.1) | copy-start | bytes 73732
  5.6 0.7 copy-start.9
  6.3 0.7 copy-start.10
  6.9 0.7 copy-start.13
  7.6 13.2 %copy-start.6 = (bf16[2,6144]{1,0:T(2,128)(2,1)S(1)}, bf16[2,6144]{1,0:T(2,128)(2,1)}, u32[]{:S(2)}) copy-start(bf16[2,6144]{1,0:T(2,128)(2,1)} %res_ref.1) | copy-start | bytes 73732
  7.6 13.2 %copy-start.11 = (s32[2,2]{1,0:T(2,128)S(1)}, s32[2,2]{1,0:T(2,128)}, u32[]{:S(2)}) copy-start(s32[2,2]{1,0:T(2,128)} %ids_ref.1) | copy-start | bytes 52
  7.6 13.2 %copy-start.12 = (f32[2,2]{1,0:T(2,128)S(1)}, f32[2,2]{1,0:T(2,128)}, u32[]{:S(2)}) copy-start(f32[2,2]{1,0:T(2,128)} %cw_ref.1) | copy-start | bytes 52
  7.6 34.0 %copy-start.7 = (f32[6144]{0:T(1024)S(1)}, f32[6144]{0:T(1024)}, u32[]{:S(2)}) copy-start(f32[6144]{0:T(1024)} %param.20) | copy-start | bytes 73732
  11.4 5.5 %collective-permute-start.2 = (bf16[112,128]{1,0:T(8,128)(2,1)S(1)}, bf16[112,128]{1,0:T(8,128)(2,1)S(1)}, u32[]{:S(2)}, u32[]{:S(2)}) collective-permute-start(bf16[112,128]{1,0:T(8,128)(2,1)S(1)} %attention.1.p0), channel_id=1, source_target_pairs={{0,64},{32,96},{64,0},{96,32},{1,65},{33,97},{65,1},{97,33},{2,66}... | collective-permute-start | bytes 86024 | tf_op jit(solution)/shard_map/ppermute | solution.py:250
  14.6 3.9 %collective-permute-start.1 = (bf16[112,128]{1,0:T(8,128)(2,1)S(1)}, bf16[112,128]{1,0:T(8,128)(2,1)S(1)}, u32[]{:S(2)}, u32[]{:S(2)}) collective-permute-start(bf16[112,128]{1,0:T(8,128)(2,1)S(1)} %attention.1.p0), channel_id=1, source_target_pairs={{0,96},{32,0},{64,32},{96,64},{1,97},{33,1},{65,33},{97,65},{2,98}... | collective-permute-start | bytes 86024 | tf_op jit(solution)/shard_map/ppermute | solution.py:250
  15.7 5.1 %collective-permute-start = (bf16[112,128]{1,0:T(8,128)(2,1)S(1)}, bf16[112,128]{1,0:T(8,128)(2,1)S(1)}, u32[]{:S(2)}, u32[]{:S(2)}) collective-permute-start(bf16[112,128]{1,0:T(8,128)(2,1)S(1)} %attention.1.p0), channel_id=1, source_target_pairs={{0,32},{32,64},{64,96},{96,0},{1,33},{33,65},{65,97},{97,1},{2,34}... | collective-permute-start | bytes 86024 | tf_op jit(solution)/shard_map/ppermute | solution.py:250
  39.7 1.8 %collective-permute-start.3 = (bf16[16,112,128]{2,1,0:T(8,128)(2,1)S(1)}, bf16[16,112,128]{2,1,0:T(8,128)(2,1)S(1)}, u32[]{:S(2)}, u32[]{:S(2)}) collective-permute-start(bf16[16,112,128]{2,1,0:T(8,128)(2,1)S(1)} %all_to_all.10.xa), channel_id=1, source_target_pairs={{0,4},{4,0},{1,5},{5,1},{2,6},{6,2},{3,7},{7,3},{8,12},{12,8},{9,1... | collective-permute-start | bytes 1376264 | tf_op jit(solution)/shard_map/ppermute | solution.py:265
  41.6 2.8 %copy-start.1 = (bf16[1,6144,512]{2,1,0:T(8,128)(2,1)S(1)}, bf16[1,6144,512]{2,1,0:T(8,128)(2,1)}, u32[]{:S(2)}) copy-start(bf16[1,6144,512]{2,1,0:T(8,128)(2,1)} %wu_hbm.1) | copy-start | bytes 18874372
  44.4 2.8 %copy-start.2 = (bf16[1,512,6144]{2,1,0:T(8,128)(2,1)S(1)}, bf16[1,512,6144]{2,1,0:T(8,128)(2,1)}, u32[]{:S(2)}) copy-start(bf16[1,512,6144]{2,1,0:T(8,128)(2,1)} %wd_hbm.1) | copy-start | bytes 18874372
  47.2 25.2 %copy-start.8 = (bf16[2,1536]{1,0:T(2,128)(2,1)S(1)}, bf16[2,1536]{1,0:T(2,128)(2,1)}, u32[]{:S(2)}) copy-start(bf16[2,1536]{1,0:T(2,128)(2,1)} %get-tuple-element.4.hid_ref) | copy-start | bytes 18436
  54.3 1.8 %collective-permute-start.4 = (bf16[1536,128]{1,0:T(8,128)(2,1)S(1)}, bf16[1536,128]{1,0:T(8,128)(2,1)S(1)}, u32[]{:S(2)}, u32[]{:S(2)}) collective-permute-start(bf16[1536,128]{1,0:T(8,128)(2,1)S(1)} %get-tuple-element.9), channel_id=1, source_target_pairs={{0,4},{4,0},{1,5},{5,1},{2,6},{6,2},{3,7},{7,3},{8,12},{12,8},{9,1... | collective-permute-start | bytes 1179656 | tf_op jit(solution)/shard_map/ppermute | solution.py:286
